TPU v7x, 128 devices: a whole 4x4x4 slice. The times are simulated.
128 devices in a mesh: band: 2 (over x_lo), brick: 64 (over z, x_hi, y, core).
Axes of the slice: x: 4 (x_hi: 2, x_lo: 2; x = x_hi * 2 + x_lo), y: 4, z: 4, core: 2. Of those that a mesh axis runs over, the one named last changes fastest.
Arguments:
- stiffness: float32 [16, 2048, 128], P('band', 'brick'), may hold values from 0.5 to 8
- prescribed: float32 [3, 16, 2048, 128], P(None, 'band', 'brick'), may hold values from -6 to 6
- pinned: int32 [16, 2048, 128], P('band', 'brick'), may hold values 0 or 1
Outputs:
- displacement: float32 [3, 16, 2048, 128], P(None, 'band', 'brick')
All inputs are finite; a program needn't handle non-finite values. No bound on the sum of `pinned` on one device may be relied on, other than what follows from the above.
Results may differ from a plain program's by a relative error of at most 0.0001.
Values sent between devices are 32-bit elements; how exact they have to be, the bound alone decides.
A program may use at most 128 MiB of HBM per device.

v0:
```python
import functools

import jax
import jax.numpy as jnp
from jax import lax
from jax.experimental import pallas as pl
from jax.experimental.pallas import tpu as pltpu
from jax.sharding import PartitionSpec as P

MESH = pl.DeviceIdType.MESH
PLANES = 13
ROWS = 72
COARSE_ROWS = 56
CHUNK = 2
BAND, OFF, DIAG_OFF, SIB, DIAG_SIB = range(5)
M_K, M_PIN, M_PR, M_KC, M_T, M_U, M_T2 = range(7)


def lane_iota():
    return lax.broadcasted_iota(jnp.int32, (1, 128), 1)


def roll(value, by):
    return pltpu.roll(value, by % 128, value.ndim - 1)


def z_pair(value, weights, step):
    low, high = weights
    return roll(value, step) * low, roll(value, -step) * high


def z_stage(field, scaled, zu, zv, dz, p, m, r0, n, weights, step):
    planes, rows = pl.ds(p, m), pl.ds(r0, n)
    for c in range(3):
        u = field[c, planes, rows]
        left, right = z_pair(u, weights, step)
        zu[c, planes, rows] = u + (left + right)
        dz[c, planes, rows] = 0.5 * (right - left)
    for c in range(3):
        v = scaled[c, planes, rows]
        left, right = z_pair(v, weights, step)
        zv[c, planes, rows] = v + (left + right)


def y_stage(field, zu, zv, dz, ep, em, ec, tv, p, m, r0, n):
    planes, mid, low, high = pl.ds(p, m), pl.ds(r0, n), pl.ds(r0 - 1, n), pl.ds(r0 + 1, n)
    for c in range(3):
        a = zu[c, planes, mid] + 0.5 * (zu[c, planes, low] + zu[c, planes, high])
        twice = a + a
        if c == 0:
            g = 0.25 * (field[1, planes, high] - field[1, planes, low]) + dz[2, planes, mid]
        elif c == 1:
            g = 0.25 * (field[0, planes, high] - field[0, planes, low])
            twice = twice + (dz[2, planes, high] - dz[2, planes, low])
        else:
            g = dz[0, planes, mid]
            twice = twice + (dz[1, planes, high] - dz[1, planes, low])
        ep[c, planes, mid] = a + g
        em[c, planes, mid] = a - g
        ec[c, planes, mid] = twice
        tv[c, planes, mid] = zv[c, planes, mid] + 0.5 * (zv[c, planes, low] + zv[c, planes, high])


def x_terms(field, k, g2, ep, em, ec, tv, c, p, m, rows):
    here, before, after = pl.ds(p, m), pl.ds(p - 1, m), pl.ds(p + 1, m)
    e = (ep[c, after, rows] + em[c, before, rows]) + ec[c, here, rows]
    mid = tv[c, here, rows]
    t = (tv[c, after, rows] + tv[c, before, rows]) + (mid + mid)
    return t + k * e - g2 * field[c, here, rows]


def kernel(
    bricks,
    stiff_in,
    pres_in,
    pin_in,
    out_hbm,
    k_own,
    k_f,
    pr_f,
    pin_f,
    g2_f,
    fh_f,
    free_f,
    fr8_f,
    ua,
    va,
    ub,
    vb,
    uc,
    ud,
    vd,
    ue,
    ve,
    res,
    out_f,
    zu,
    zv,
    dz,
    ep,
    em,
    ec,
    tv,
    prolonged,
    kc_b,
    kc_off,
    kc_sib,
    kt,
    t_b,
    t_off,
    t_sib,
    t2_b,
    t2_sib,
    tt,
    k_q,
    g_q,
    s_q,
    w_q,
    ca,
    cva,
    cb,
    cvb,
    czu,
    czv,
    cdz,
    cep,
    cem,
    cec,
    ctv,
    in_sem,
    send_sem,
    recv_sem,
):
    b = lax.axis_index("band")
    i = lax.axis_index("brick")
    c = lax.rem(i, 2)
    has_off = ((c == 0) & (i > 0)) | ((c == 1) & (i < bricks - 1))
    i_off = i - 1 + 2 * c
    i_sib = i + 1 - 2 * c
    own_row = pl.multiple_of(24 - 8 * c, 8)
    own_plane = 1 + 3 * b
    partners = {BAND: (1 - b, i), OFF: (b, i_off), DIAG_OFF: (1 - b, i_off), SIB: (b, i_sib), DIAG_SIB: (1 - b, i_sib)}

    locals_ = [
        pltpu.make_async_copy(stiff_in, k_f.at[pl.ds(own_plane, 8), pl.ds(own_row, 32)], in_sem.at[0]),
        pltpu.make_async_copy(pin_in, pin_f.at[pl.ds(own_plane, 8), pl.ds(own_row, 32)], in_sem.at[1]),
        pltpu.make_async_copy(pres_in, pr_f.at[:, pl.ds(own_plane, 8), pl.ds(own_row, 32)], in_sem.at[2]),
        pltpu.make_async_copy(stiff_in, k_own.at[:, pl.ds(own_row, 32)], in_sem.at[4]),
    ]
    for copy in locals_:
        copy.start()
    barrier = pltpu.get_barrier_semaphore()

    def greet(kind):
        pl.semaphore_signal(barrier, inc=1, device_id=partners[kind], device_id_type=MESH)

    for kind in (BAND, SIB, DIAG_SIB):
        greet(kind)

    @pl.when(has_off)
    def _():
        greet(OFF)
        greet(DIAG_OFF)

    @pl.when(jnp.logical_not(has_off))
    def _():
        deep = pl.ds(pl.multiple_of(8 + 40 * c, 8), 16)
        plain = jnp.zeros((PLANES, 16, 128), jnp.float32)
        k_f[:, deep] = plain
        pin_f[:, deep] = jnp.zeros((PLANES, 16, 128), jnp.int32)
        for comp in range(3):
            pr_f[comp, :, deep] = plain
            uc[comp, :, deep] = plain
        kc_off[...] = jnp.zeros(kc_off.shape, jnp.float32)
        t_off[...] = jnp.zeros(t_off.shape, jnp.float32)

    outer = 12 * b
    k_f[outer] = jnp.zeros((ROWS, 128), jnp.float32)
    for ref in (ep, em, tv):
        for comp in range(3):
            ref[comp, outer] = jnp.zeros((ROWS, 128), jnp.float32)
    edge = pl.ds(16, 24)
    for comp in range(3):
        for half in range(2):
            t_b[0, comp, half, edge] = jnp.zeros((24, 128), jnp.float32)
            t2_b[0, comp, half, edge] = jnp.zeros((24, 128), jnp.float32)
    for half in range(2):
        kc_b[0, half, edge] = jnp.zeros((24, 128), jnp.float32)

    lane = lane_iota()
    even = lax.rem(lane, 2) == 0
    fine_w = (jnp.where(lane == 0, 0.0, 0.5), jnp.where(lane == 127, 0.0, 0.5))
    coarse_w = (jnp.where(lane < 2, 0.0, 0.5), jnp.where(lane >= 126, 0.0, 0.5))
    first_core = lax.broadcasted_iota(jnp.int32, (8, 128), 0) * 0 + c == 0

    def by_core(zero, one):
        return jnp.where(first_core[: zero.shape[0]], zero, one)

    def halve(load, dst):
        sums = []
        for x in range(4):
            p = 2 * x
            top, low = pl.ds(16, 20, stride=2), pl.ds(17, 20, stride=2)
            sums.append((load(p, top) + load(p, low)) + (load(p + 1, top) + load(p + 1, low)))
        for half in range(2):
            first, second = sums[half], sums[half + 2]
            dst(half, jnp.where(even, first + roll(first, -1), second + roll(second, 1)))

    locals_[3].wait()

    def put_kc(half, value):
        kc_b[0, half, pl.ds(20, 20)] = 0.125 * value

    halve(lambda p, rows: k_own[p, rows], put_kc)

    copies = {}

    def prepare(message, kind, src, dst):
        copies[message, kind] = pltpu.make_async_remote_copy(
            src_ref=src,
            dst_ref=dst,
            send_sem=send_sem.at[message, kind],
            recv_sem=recv_sem.at[message, kind],
            device_id=partners[kind],
            device_id_type=MESH,
        )

    def fine_messages(message, src, dst, lead, src_plane, src_row, off_rows, depth):
        pick = (lambda ref, planes, rows: ref.at[:, planes, rows]) if lead else (lambda ref, planes, rows: ref.at[planes, rows])
        all_s, all_d = pl.ds(src_plane, 8), pl.ds(own_plane, 8)
        face_s = pl.ds(src_plane + (8 - depth) * (1 - b), depth)
        face_d = pl.ds((4 - depth) * (1 - b) + 9 * b, depth)
        rows_s = pl.ds(pl.multiple_of(src_row, 8), 32)
        off_s = pl.ds(pl.multiple_of(src_row + (32 - off_rows) * c, 8), off_rows)
        off_d = pl.ds(pl.multiple_of(48 * (1 - c) + (24 - off_rows) * c, 8), off_rows)
        sib_s = pl.ds(pl.multiple_of(src_row + 24 * (1 - c), 8), 8)
        sib_d = pl.ds(pl.multiple_of(8 + 48 * c, 8), 8)
        prepare(message, OFF, pick(src, all_s, off_s), pick(dst, all_d, off_d))
        prepare(message, DIAG_OFF, pick(src, face_s, off_s), pick(dst, face_d, off_d))
        prepare(message, BAND, pick(src, face_s, rows_s), pick(dst, face_d, pl.ds(own_row, 32)))
        prepare(message, SIB, pick(src, all_s, sib_s), pick(dst, all_d, sib_d))
        prepare(message, DIAG_SIB, pick(src, face_s, sib_s), pick(dst, face_d, sib_d))

    def coarse_messages(message, held, off, sib):
        lead = (slice(None),) * (len(held.shape) - 3)

        def rows(ref, slot, start, count):
            return ref.at[(slot, *lead, pl.ds(start, count))]

        sib_row = pl.multiple_of(24 - 8 * c, 8)
        prepare(message, OFF, rows(held, 0, 24, 16), off.at[0])
        prepare(message, DIAG_OFF, rows(held, 0, 24, 16), off.at[1])
        prepare(message, BAND, rows(held, 0, 16, 24), rows(held, 1, 16, 24))
        prepare(message, SIB, rows(held, 0, sib_row, 16), sib.at[0])
        prepare(message, DIAG_SIB, rows(held, 0, sib_row, 16), sib.at[1])

    fine_messages(M_PR, pres_in, pr_f, True, 0, 0, 8, 2)
    fine_messages(M_K, stiff_in, k_f, False, 0, 0, 16, 3)
    fine_messages(M_PIN, pin_in, pin_f, False, 0, 0, 16, 3)
    coarse_messages(M_KC, kc_b, kc_off, kc_sib)
    coarse_messages(M_T, t_b, t_off, t_sib)
    fine_messages(M_U, uc, uc, True, own_plane, own_row, 16, 3)
    block = pl.ds(pl.multiple_of(32 - 16 * c, 8), 8)
    prepare(M_T2, BAND, t2_b.at[0, :, :, pl.ds(16, 24)], t2_b.at[1, :, :, pl.ds(16, 24)])
    prepare(M_T2, SIB, t2_b.at[0, :, :, block], t2_sib.at[0])
    prepare(M_T2, DIAG_SIB, t2_b.at[0, :, :, block], t2_sib.at[1])

    def each(messages, act, off=True):
        if off:

            @pl.when(has_off)
            def _():
                for kind in (OFF, DIAG_OFF):
                    for message in messages:
                        act(copies[message, kind])

        for kind in (BAND, DIAG_SIB, SIB):
            for message in messages:
                act(copies[message, kind])

    def start(*messages, off=True):
        each(messages, lambda copy: copy.start(), off)

    def received(*messages, off=True):
        each(messages, lambda copy: copy.wait_recv(), off)

    def sent(*messages, off=True):
        each(messages, lambda copy: copy.wait_send(), off)

    pl.semaphore_wait(barrier, 3 + 2 * has_off.astype(jnp.int32))
    start(M_PR, M_K, M_PIN)
    start(M_KC)

    locals_[0].wait()
    locals_[1].wait()
    locals_[2].wait()
    received(M_PR, M_K, M_PIN)

    def begin(p, m, r0, n):
        planes, rows = pl.ds(p, m), pl.ds(r0, n)
        pinned = pin_f[planes, rows].astype(jnp.float32)
        k = k_f[planes, rows]
        for comp in range(3):
            u = pr_f[comp, planes, rows] * pinned
            ua[comp, planes, rows] = u
            va[comp, planes, rows] = k * u

    for q in range(0, 10, CHUNK):
        begin(1 + b + q, CHUNK, 14, 44)

    for p in range(1, 12):
        k = k_f[p, pl.ds(13, 46)]
        left, right = z_pair(k, fine_w, 1)
        zu[0, p, pl.ds(13, 46)] = k + (left + right)
    for p in range(1, 12):
        tv[0, p, pl.ds(14, 44)] = zu[0, p, pl.ds(14, 44)] + 0.5 * (zu[0, p, pl.ds(13, 44)] + zu[0, p, pl.ds(15, 44)])
    for p in range(1, 12):
        free = 1.0 - pin_f[p, pl.ds(13, 46)].astype(jnp.float32)
        free_f[p, pl.ds(13, 46)] = free
        fr8_f[p, pl.ds(13, 46)] = 0.0625 * free
    for q in range(10):
        p, rows = 1 + b + q, pl.ds(14, 44)
        k = k_f[p, rows]
        t = tv[0, p, rows] + 0.5 * (tv[0, p - 1, rows] + tv[0, p + 1, rows])
        g2_f[p, rows] = 16.0 * k + 2.0 * t
        diagonal = 6.0 * k + t
        fh_f[p, rows] = jnp.where(k > 0.0, 0.3 * free_f[p, rows] / jnp.where(k > 0.0, diagonal, 1.0), 0.0)

    def fine(field, scaled, p, m, out_p, out_m, r0, n, emit):
        for q in range(0, m, CHUNK):
            size = min(CHUNK, m - q)
            z_stage(field, scaled, zu, zv, dz, p + q, size, r0 - 1, n + 2, fine_w, 1)
            y_stage(field, zu, zv, dz, ep, em, ec, tv, p + q, size, r0, n)
        rows = pl.ds(r0, n)
        for done in range(0, out_m, CHUNK):
            size = min(CHUNK, out_m - done)
            at = out_p + done
            here = pl.ds(at, size)
            k, g2 = k_f[here, rows], g2_f[here, rows]
            for comp in range(3):
                emit(comp, here, rows, k, field, x_terms(field, k, g2, ep, em, ec, tv, comp, at, size, rows))

    def sweep_to(out_u, out_v):
        def emit(comp, here, rows, k, field, terms):
            u = field[comp, here, rows] + fh_f[here, rows] * terms
            out_u[comp, here, rows] = u
            if out_v is not None:
                out_v[comp, here, rows] = u * k

        return emit

    def to_residual(comp, here, rows, k, field, terms):
        res[comp, here, rows] = fr8_f[here, rows] * terms

    def sweep_wide(field, scaled, out_u, out_v):
        fine(field, scaled, 1, 11, 1 + b, 10, 14, 44, sweep_to(out_u, out_v))

    def sweep_near(field, scaled, out_u, out_v):
        fine(field, scaled, 1 + b, 10, 1 + 2 * b, 9, 15, 42, sweep_to(out_u, out_v))

    def residual(field, scaled):
        fine(field, scaled, 1 + 2 * b, 9, own_plane, 8, 16, 40, to_residual)

    sweep_near(ua, va, ub, vb)
    own = (pl.ds(own_plane, 8), pl.ds(own_row, 32))
    for comp in range(3):
        uc[(comp, *own)] = ub[(comp, *own)]
    residual(ub, vb)

    def put_target(dst):
        for comp in range(3):

            def put(half, value, comp=comp):
                dst[0, comp, half, pl.ds(20, 20)] = value

            halve(lambda p, rows, comp=comp: res[comp, own_plane + p, rows], put)

    put_target(t_b)
    start(M_T)
    start(M_U)

    def assemble(held, off, sib, dst):
        dst[pl.ds(24, 12)] = held[pl.ds(24, 12)]
        dst[pl.ds(14, 6)] = by_core(off[pl.ds(2, 6)], sib[pl.ds(10, 6)])
        dst[pl.ds(20, 4)] = by_core(off[pl.ds(8, 4)], held[pl.ds(20, 4)])
        dst[pl.ds(36, 4)] = by_core(held[pl.ds(36, 4)], off[pl.ds(0, 4)])
        dst[pl.ds(40, 6)] = by_core(sib[pl.ds(4, 6)], off[pl.ds(4, 6)])

    def repack(load, rows, emit):
        for half in range(2):
            low, high = load(b, half, rows), load(1 - b, half, rows)
            emit(1 + half, jnp.where(even, low, roll(high, 1)))
            emit(3 + half, jnp.where(even, roll(low, -1), high))

    received(M_KC)
    for slot in range(2):
        for half in range(2):
            assemble(kc_b.at[slot, half], kc_off.at[slot, half], kc_sib.at[slot, half], kt.at[slot, half])

    def put_kq(q, value):
        k_q[q, pl.ds(14, 32)] = value

    repack(lambda slot, half, rows: kt[slot, half, rows], pl.ds(14, 32), put_kq)

    def wrap_after(value):
        return jnp.where(even, roll(value, -1), 0.0)

    def wrap_before(value):
        return jnp.where(even, 0.0, roll(value, 1))

    for q in range(1, 5):
        k = k_q[q, pl.ds(14, 32)]
        left, right = z_pair(k, coarse_w, 2)
        czu[0, q, pl.ds(14, 32)] = k + (left + right)
    whole = pl.ds(15, 30)
    for q in range(1, 5):
        ctv[0, q, whole] = czu[0, q, whole] + 0.5 * (czu[0, q, pl.ds(14, 30)] + czu[0, q, pl.ds(16, 30)])
    ctv[0, 5, whole] = wrap_after(ctv[0, 1, whole])
    ctv[0, 0, whole] = wrap_before(ctv[0, 4, whole])
    for q in range(1, 5):
        k = k_q[q, whole]
        t = ctv[0, q, whole] + 0.5 * (ctv[0, q - 1, whole] + ctv[0, q + 1, whole])
        g_q[q, whole] = 16.0 * k + 2.0 * t
        s_q[q, whole] = jnp.where(k > 0.0, 0.3 / jnp.where(k > 0.0, 6.0 * k + t, 1.0), 0.0)

    def coarse_sweep(field, scaled, out_u, out_v, r0, n):
        z_stage(field, scaled, czu, czv, cdz, 1, 4, r0 - 1, n + 2, coarse_w, 2)
        y_stage(field, czu, czv, cdz, cep, cem, cec, ctv, 1, 4, r0, n)
        rows = pl.ds(r0, n)
        for comp in range(3):
            cep[comp, 5, rows] = wrap_after(cep[comp, 1, rows])
            cem[comp, 0, rows] = wrap_before(cem[comp, 4, rows])
            ctv[comp, 5, rows] = wrap_after(ctv[comp, 1, rows])
            ctv[comp, 0, rows] = wrap_before(ctv[comp, 4, rows])
        here = pl.ds(1, 4)
        k, g2, s = k_q[here, rows], g_q[here, rows], s_q[here, rows]
        for comp in range(3):
            terms = x_terms(field, k, g2, cep, cem, cec, ctv, comp, 1, 4, rows)
            u = field[comp, here, rows] + (w_q[comp, here, rows] + s * terms)
            out_u[comp, here, rows] = u
            if out_v is not None:
                out_v[comp, here, rows] = u * k

    def coarse(load, r0, n):
        rows = pl.ds(r0, n)
        for comp in range(3):

            def put(q, value, comp=comp):
                w = 8.0 * s_q[q, rows] * value
                w_q[comp, q, rows] = w
                ca[comp, q, rows] = w
                cva[comp, q, rows] = w * k_q[q, rows]

            repack(lambda slot, half, at, comp=comp: load(slot, comp, half, at), rows, put)
        coarse_sweep(ca, cva, cb, cvb, r0 + 1, n - 2)
        coarse_sweep(cb, cvb, ca, cva, r0 + 2, n - 4)
        coarse_sweep(ca, cva, cb, None, r0 + 3, n - 6)
        last, count = r0 + 3, n - 6
        for comp in range(3):
            for q in range(1, 5):
                value = cb[comp, q, pl.ds(last, count)]
                for x, part in ((q - 1, jnp.where(even, value, roll(value, 1))), (q + 3, jnp.where(even, roll(value, -1), value))):
                    prolonged[comp, x, pl.ds(2 * last - 24, count, stride=2)] = part
                    prolonged[comp, x, pl.ds(2 * last - 23, count, stride=2)] = part

    def correct(field, out_u, out_v, p, m, r0, n):
        rows = pl.ds(r0, n)
        for q in range(m):
            at = p + q
            x = (at - 1 + 5 * b) // 2
            k, free = k_f[at, rows], free_f[at, rows]
            for comp in range(3):
                u = field[comp, at, rows] + free * prolonged[comp, x, rows]
                out_u[comp, at, rows] = u
                out_v[comp, at, rows] = u * k

    received(M_T)
    for slot in range(2):
        for comp in range(3):
            for half in range(2):
                assemble(
                    t_b.at[slot, comp, half], t_off.at[slot, comp, half], t_sib.at[slot, comp, half], tt.at[slot, comp, half]
                )
    coarse(lambda slot, comp, half, rows: tt[slot, comp, half, rows], 15, 30)
    received(M_U)
    correct(uc, ud, vd, 1, 11, 13, 46)
    sweep_wide(ud, vd, ue, ve)

    sweep_near(ue, ve, ud, vd)
    residual(ud, vd)
    put_target(t2_b)
    start(M_T2, off=False)
    received(M_T2, off=False)
    for slot in range(2):
        for comp in range(3):
            for half in range(2):
                tt[slot, comp, half, pl.ds(16, 24)] = t2_b[slot, comp, half, pl.ds(16, 24)]
                near = t2_sib[slot, comp, half, pl.ds(4, 4)]
                tt[slot, comp, half, pl.ds(16, 4)] = near
                tt[slot, comp, half, pl.ds(40, 4)] = near
    coarse(lambda slot, comp, half, rows: tt[slot, comp, half, rows], 16, 28)
    correct(ud, ue, ve, 1 + 2 * b, 9, 15, 42)
    fine(ue, ve, 1 + 2 * b, 9, own_plane, 8, 16, 40, sweep_to(out_f, None))
    result = pltpu.make_async_copy(out_f.at[(slice(None), *own)], out_hbm, in_sem.at[3])
    result.start()
    sent(M_PR, M_K, M_PIN, M_KC, M_T, M_U)
    sent(M_T2, off=False)
    result.wait()


def solution(mesh):
    bricks = mesh.shape["brick"]

    def body(stiffness, prescribed, pinned):
        def f32(*shape):
            return pltpu.VMEM(shape, jnp.float32)

        one, three = f32(PLANES, ROWS, 128), f32(3, PLANES, ROWS, 128)
        q1, q3 = f32(6, COARSE_ROWS, 128), f32(3, 6, COARSE_ROWS, 128)
        scratch = [
            f32(8, ROWS, 128),
            one,
            three,
            pltpu.VMEM((PLANES, ROWS, 128), jnp.int32),
            *[one] * 4,
            *[three] * 11,
            *[three] * 7,
            f32(3, 8, ROWS, 128),
            f32(2, 2, COARSE_ROWS, 128),
            f32(2, 2, 16, 128),
            f32(2, 2, 16, 128),
            f32(2, 2, COARSE_ROWS, 128),
            f32(2, 3, 2, COARSE_ROWS, 128),
            f32(2, 3, 2, 16, 128),
            f32(2, 3, 2, 16, 128),
            f32(2, 3, 2, COARSE_ROWS, 128),
            f32(2, 3, 2, 8, 128),
            f32(2, 3, 2, COARSE_ROWS, 128),
            *[q1] * 3,
            *[q3] * 5,
            *[q3] * 7,
            pltpu.SemaphoreType.DMA((5,)),
            pltpu.SemaphoreType.DMA((7, 5)),
            pltpu.SemaphoreType.DMA((7, 5)),
        ]
        hbm = pl.BlockSpec(memory_space=pl.ANY)
        return pl.pallas_call(
            functools.partial(kernel, bricks),
            out_shape=jax.ShapeDtypeStruct(prescribed.shape, jnp.float32),
            in_specs=[hbm] * 3,
            out_specs=hbm,
            scratch_shapes=scratch,
            compiler_params=pltpu.CompilerParams(collective_id=0, has_side_effects=True, vmem_limit_bytes=58 * 2**20),
        )(stiffness, prescribed, pinned)

    return jax.shard_map(
        body,
        mesh=mesh,
        in_specs=(P("band", "brick", None), P(None, "band", "brick", None), P("band", "brick", None)),
        out_specs=P(None, "band", "brick", None),
        check_vma=False,
    )
```

profile of v0, /device:TPU:32, one launch (start us, length us, event | category | flops | bytes accessed | tf_op | source)
XLA Modules:
  0.0 43.2 jit_solution(14906694830404796270)
XLA Ops:
  0.0 41.4 %shard_map.37 = f32[3,8,32,128]{3,2,1,0:T(8,128)} custom-call(f32[8,32,128]{2,1,0:T(8,128)} %stiff_in.1, f32[3,8,32,128]{3,2,1,0:T(8,128)} %pres_in.1, s32[8,32,128]{2,1,0:T(8,128)} %pin_in.1), custom_call_target="tpu_custom_call" | custom-call | tf_op jit(solution)/shard_map/pallas_call | solution.py:547
  41.5 1.8 %copy.5 = f32[3,8,32,128]{3,2,1,0:T(8,128)} copy(f32[3,8,32,128]{3,2,1,0:T(8,128)} %shard_map.37) | data formatting | bytes 786432
where the time goes:
time: 43.7 us; the launch traced here: 43.2 us
  Pallas kernels  41.4 us (95%)
  local copies, waits for them, and re-layouts  1.77 us (4%)
    pallas_call x1, Pallas kernels, body(): pl.pallas_call(functools.partial(kernel, bricks), out_shape=jax.ShapeDtyp...  41.4 us
    unnamed x1, local copies, waits for them, and re-layouts  1.77 us

commit v1 on v0

v1 whole, which is shorter than its diff:
```python
import functools

import jax
import jax.numpy as jnp
from jax import lax
from jax.experimental import pallas as pl
from jax.experimental.pallas import tpu as pltpu
from jax.sharding import PartitionSpec as P

MESH = pl.DeviceIdType.MESH
PLANES = 13
ROWS = 48
COARSE_ROWS = 32
CHUNK = 2
BAND, UP, DOWN, DIAG_UP, DIAG_DOWN = range(5)
MESSAGES = 8
M_IN, M_FACE_U, M_FACE_K, M_FACE_FREE, M_KC, M_T, M_U, M_T2 = range(MESSAGES)


def lane_iota():
    return lax.broadcasted_iota(jnp.int32, (1, 128), 1)


def roll(value, by):
    return pltpu.roll(value, by % 128, value.ndim - 1)


def z_pair(value, weights, step):
    low, high = weights
    return roll(value, step) * low, roll(value, -step) * high


def z_stage(field, scaled, zu, zv, dz, p, m, r0, n, weights, step):
    planes, rows = pl.ds(p, m), pl.ds(r0, n)
    for c in range(3):
        u = field[c, planes, rows]
        left, right = z_pair(u, weights, step)
        zu[c, planes, rows] = u + (left + right)
        dz[c, planes, rows] = 0.5 * (right - left)
    for c in range(3):
        v = scaled[c, planes, rows]
        left, right = z_pair(v, weights, step)
        zv[c, planes, rows] = v + (left + right)


def y_stage(field, zu, zv, dz, ep, em, ec, tv, p, m, r0, n):
    planes, mid, low, high = pl.ds(p, m), pl.ds(r0, n), pl.ds(r0 - 1, n), pl.ds(r0 + 1, n)
    for c in range(3):
        a = zu[c, planes, mid] + 0.5 * (zu[c, planes, low] + zu[c, planes, high])
        twice = a + a
        if c == 0:
            g = 0.25 * (field[1, planes, high] - field[1, planes, low]) + dz[2, planes, mid]
        elif c == 1:
            g = 0.25 * (field[0, planes, high] - field[0, planes, low])
            twice = twice + (dz[2, planes, high] - dz[2, planes, low])
        else:
            g = dz[0, planes, mid]
            twice = twice + (dz[1, planes, high] - dz[1, planes, low])
        ep[c, planes, mid] = a + g
        em[c, planes, mid] = a - g
        ec[c, planes, mid] = twice
        tv[c, planes, mid] = zv[c, planes, mid] + 0.5 * (zv[c, planes, low] + zv[c, planes, high])


def x_terms(field, k, g2, ep, em, ec, tv, c, p, m, rows):
    here, before, after = pl.ds(p, m), pl.ds(p - 1, m), pl.ds(p + 1, m)
    e = (ep[c, after, rows] + em[c, before, rows]) + ec[c, here, rows]
    mid = tv[c, here, rows]
    t = (tv[c, after, rows] + tv[c, before, rows]) + (mid + mid)
    return t + k * e - g2 * field[c, here, rows]


def kernel(
    bricks,
    stiff_in,
    pres_in,
    pin_in,
    out_hbm,
    pr_in,
    pin_own,
    k_own,
    k_f,
    free_f,
    fr8_f,
    g2_f,
    fh_f,
    ua,
    va,
    ub,
    vb,
    uc,
    ud,
    vd,
    ue,
    ve,
    res,
    out_f,
    zu,
    zv,
    dz,
    ep,
    em,
    ec,
    tv,
    prolonged,
    in_pack,
    in_land,
    in_diag_pack,
    in_diag_land,
    u_pack,
    u_land,
    u_diag_pack,
    u_diag_land,
    kc,
    t_1,
    t_2,
    k_q,
    g_q,
    s_q,
    w_q,
    ca,
    cva,
    cb,
    cvb,
    czu,
    czv,
    cdz,
    cep,
    cem,
    cec,
    ctv,
    in_sem,
    send_sem,
    recv_sem,
):
    b = lax.axis_index("band")
    i = lax.axis_index("brick")
    has_up, has_down = i > 0, i < bricks - 1
    own_plane = 1 + 3 * b
    planes_own = pl.ds(own_plane, 8)
    partners = {BAND: (1 - b, i), UP: (b, i - 1), DOWN: (b, i + 1), DIAG_UP: (1 - b, i - 1), DIAG_DOWN: (1 - b, i + 1)}

    locals_ = [
        pltpu.make_async_copy(stiff_in, k_own, in_sem.at[0]),
        pltpu.make_async_copy(pin_in, pin_own, in_sem.at[1]),
        pltpu.make_async_copy(pres_in, pr_in, in_sem.at[2]),
    ]
    for copy in locals_:
        copy.start()
    barrier = pltpu.get_barrier_semaphore()

    def greet(kind):
        pl.semaphore_signal(barrier, inc=1, device_id=partners[kind], device_id_type=MESH)

    greet(BAND)

    @pl.when(has_up)
    def _():
        greet(UP)
        greet(DIAG_UP)

    @pl.when(has_down)
    def _():
        greet(DOWN)
        greet(DIAG_DOWN)

    def outside(slot, rows):
        for ref in (in_land, in_diag_land, u_land, u_diag_land):
            ref[slot] = jnp.zeros(ref.shape[1:], jnp.float32)
        for band in range(2):
            for half in range(2):
                kc[band, half, rows] = jnp.zeros((8, 128), jnp.float32)
                for comp in range(3):
                    t_1[band, comp, half, rows] = jnp.zeros((8, 128), jnp.float32)
                    t_2[band, comp, half, rows] = jnp.zeros((8, 128), jnp.float32)

    @pl.when(jnp.logical_not(has_up))
    def _():
        outside(1, pl.ds(0, 8))

    @pl.when(jnp.logical_not(has_down))
    def _():
        outside(0, pl.ds(24, 8))

    outer = 12 * b
    k_f[outer] = jnp.zeros((ROWS, 128), jnp.float32)
    for ref in (ep, em, tv):
        for comp in range(3):
            ref[comp, outer] = jnp.zeros((ROWS, 128), jnp.float32)

    lane = lane_iota()
    even = lax.rem(lane, 2) == 0
    fine_w = (jnp.where(lane == 0, 0.0, 0.5), jnp.where(lane == 127, 0.0, 0.5))
    coarse_w = (jnp.where(lane < 2, 0.0, 0.5), jnp.where(lane >= 126, 0.0, 0.5))

    def halve(load, first_row, emit):
        sums = []
        for x in range(4):
            p = 2 * x
            top, low = pl.ds(first_row, 16, stride=2), pl.ds(first_row + 1, 16, stride=2)
            sums.append((load(p, top) + load(p, low)) + (load(p + 1, top) + load(p + 1, low)))
        for half in range(2):
            first, second = sums[half], sums[half + 2]
            emit(half, jnp.where(even, first + roll(first, -1), second + roll(second, 1)))

    copies = {}

    def prepare(message, kind, src, dst):
        copies[message, kind] = pltpu.make_async_remote_copy(
            src_ref=src,
            dst_ref=dst,
            send_sem=send_sem.at[message, kind],
            recv_sem=recv_sem.at[message, kind],
            device_id=partners[kind],
            device_id_type=MESH,
        )

    def face_message(message, ref, depth, lead):
        src, dst = pl.ds(4 + (5 - depth) * (1 - b), depth), pl.ds((4 - depth) * (1 - b) + 9 * b, depth)
        rows = pl.ds(8, 32)
        if lead:
            prepare(message, BAND, ref.at[:, src, rows], ref.at[:, dst, rows])
        else:
            prepare(message, BAND, ref.at[src, rows], ref.at[dst, rows])

    def packed_messages(message, pack, land, diag_pack, diag_land):
        for slot, near, far in ((0, UP, DIAG_UP), (1, DOWN, DIAG_DOWN)):
            prepare(message, near, pack.at[slot], land.at[slot])
            prepare(message, far, diag_pack.at[slot], diag_land.at[slot])

    def coarse_messages(message, ref):
        def at(band, start, count):
            if len(ref.shape) == 4:
                return ref.at[band, :, pl.ds(start, count)]
            return ref.at[band, :, :, pl.ds(start, count)]

        prepare(message, BAND, at(0, 8, 16), at(1, 8, 16))
        prepare(message, UP, at(0, 8, 8), at(0, 24, 8))
        prepare(message, DIAG_UP, at(0, 8, 8), at(1, 24, 8))
        prepare(message, DOWN, at(0, 16, 8), at(0, 0, 8))
        prepare(message, DIAG_DOWN, at(0, 16, 8), at(1, 0, 8))

    packed_messages(M_IN, in_pack, in_land, in_diag_pack, in_diag_land)
    face_message(M_FACE_U, ua, 2, True)
    face_message(M_FACE_K, k_f, 3, False)
    face_message(M_FACE_FREE, free_f, 3, False)
    coarse_messages(M_KC, kc)
    coarse_messages(M_T, t_1)
    coarse_messages(M_T2, t_2)
    packed_messages(M_U, u_pack, u_land, u_diag_pack, u_diag_land)
    face_message(M_U, uc, 3, True)

    def each(messages, act, above, below):
        for holds, kinds in ((above, (UP, DIAG_UP)), (below, (DOWN, DIAG_DOWN))):
            found = [copies[m, kind] for m in messages for kind in kinds if (m, kind) in copies]
            if found:

                @pl.when(holds)
                def _(found=found):
                    for copy in found:
                        act(copy)

        for m in messages:
            if (m, BAND) in copies:
                act(copies[m, BAND])

    def start(*messages):
        each(messages, lambda copy: copy.start(), has_up, has_down)

    def received(*messages):
        each(messages, lambda copy: copy.wait_recv(), has_down, has_up)

    def sent(*messages):
        each(messages, lambda copy: copy.wait_send(), has_up, has_down)

    def edges(slot, depth):
        return (pl.ds(8, depth), pl.ds(40, depth)) if slot == 0 else (pl.ds(40 - depth, depth), pl.ds(8 - depth, depth))

    def pack(fields, dst, diag_dst):
        total = sum(depth for _, depth in fields)
        face = own_plane + 5 * (1 - b)
        for slot in range(2):
            at = 0
            for load, depth in fields:
                rows = edges(slot, depth)[0]
                for q in range(8):
                    dst[slot, pl.ds(q * total + at, depth)] = load(own_plane + q, rows)
                for q in range(3):
                    diag_dst[slot, pl.ds(q * total + at, depth)] = load(face + q, rows)
                at += depth

    def unpack(fields, land, diag_land):
        total = sum(depth for _, depth in fields)
        face = 1 + 8 * (1 - b)
        for slot in range(2):
            at = 0
            for store, depth in fields:
                rows = edges(slot, depth)[1]
                for q in range(8):
                    store(own_plane + q, rows, land[slot, pl.ds(q * total + at, depth)])
                for q in range(3):
                    store(face + q, rows, diag_land[slot, pl.ds(q * total + at, depth)])
                at += depth

    def load_of(ref, comp=None):
        return (lambda p, rows: ref[p, rows]) if comp is None else (lambda p, rows: ref[comp, p, rows])

    def store_of(ref, comp=None):
        def store(p, rows, value):
            if comp is None:
                ref[p, rows] = value
            else:
                ref[comp, p, rows] = value

        return store

    for copy in locals_:
        copy.wait()
    own_rows = pl.ds(8, 32)
    for q in range(8):
        at = own_plane + q
        pinned = pin_own[q].astype(jnp.float32)
        free_f[at, own_rows] = 1.0 - pinned
        k = k_own[q]
        k_f[at, own_rows] = k
        for comp in range(3):
            u = pr_in[comp, q] * pinned
            ua[comp, at, own_rows] = u
            va[comp, at, own_rows] = k * u
    pack(
        [(load_of(ua, 0), 2), (load_of(ua, 1), 2), (load_of(ua, 2), 2), (load_of(k_f), 3), (load_of(free_f), 3)],
        in_pack,
        in_diag_pack,
    )

    def put_kc(half, value):
        kc[0, half, pl.ds(8, 16)] = 0.125 * value

    halve(lambda p, rows: k_own[p, rows], 0, put_kc)

    pl.semaphore_wait(barrier, 1 + 2 * has_up.astype(jnp.int32) + 2 * has_down.astype(jnp.int32))
    start(M_IN, M_FACE_U, M_FACE_K, M_FACE_FREE)
    start(M_KC)
    received(M_IN, M_FACE_U, M_FACE_K, M_FACE_FREE)
    unpack(
        [(store_of(ua, 0), 2), (store_of(ua, 1), 2), (store_of(ua, 2), 2), (store_of(k_f), 3), (store_of(free_f), 3)],
        in_land,
        in_diag_land,
    )
    near = pl.ds(6, 36)
    for q in range(10):
        at = 1 + b + q
        k = k_f[at, near]
        for comp in range(3):
            va[comp, at, near] = k * ua[comp, at, near]

    for p in range(1, 12):
        k = k_f[p, pl.ds(5, 38)]
        left, right = z_pair(k, fine_w, 1)
        zu[0, p, pl.ds(5, 38)] = k + (left + right)
        fr8_f[p, own_rows] = 0.0625 * free_f[p, own_rows]
    for p in range(1, 12):
        tv[0, p, near] = zu[0, p, near] + 0.5 * (zu[0, p, pl.ds(5, 36)] + zu[0, p, pl.ds(7, 36)])
    for q in range(10):
        p = 1 + b + q
        k = k_f[p, near]
        t = tv[0, p, near] + 0.5 * (tv[0, p - 1, near] + tv[0, p + 1, near])
        g2_f[p, near] = 16.0 * k + 2.0 * t
        diagonal = 6.0 * k + t
        fh_f[p, near] = jnp.where(k > 0.0, 0.3 * free_f[p, near] / jnp.where(k > 0.0, diagonal, 1.0), 0.0)

    def fine(field, scaled, p, m, out_p, out_m, r0, n, emit):
        rows = pl.ds(r0, n)
        done = 0
        for q in range(0, m, CHUNK):
            size = min(CHUNK, m - q)
            z_stage(field, scaled, zu, zv, dz, p + q, size, r0 - 1, n + 2, fine_w, 1)
            y_stage(field, zu, zv, dz, ep, em, ec, tv, p + q, size, r0, n)
            while done < out_m:
                out_size = min(CHUNK, out_m - done)
                if q + size < min(m, done + out_size + 2):
                    break
                at = out_p + done
                here = pl.ds(at, out_size)
                k, g2 = k_f[here, rows], g2_f[here, rows]
                for comp in range(3):
                    emit(comp, here, rows, k, field, x_terms(field, k, g2, ep, em, ec, tv, comp, at, out_size, rows))
                done += out_size

    def sweep_to(out_u, out_v):
        def emit(comp, here, rows, k, field, terms):
            u = field[comp, here, rows] + fh_f[here, rows] * terms
            out_u[comp, here, rows] = u
            if out_v is not None:
                out_v[comp, here, rows] = u * k

        return emit

    def to_residual(comp, here, rows, k, field, terms):
        res[comp, here, rows] = fr8_f[here, rows] * terms

    def sweep_wide(field, scaled, out_u, out_v):
        fine(field, scaled, 1, 11, 1 + b, 10, 6, 36, sweep_to(out_u, out_v))

    def sweep_near(field, scaled, out_u, out_v):
        fine(field, scaled, 1 + b, 10, 1 + 2 * b, 9, 7, 34, sweep_to(out_u, out_v))

    def residual(field, scaled):
        fine(field, scaled, 1 + 2 * b, 9, own_plane, 8, 8, 32, to_residual)

    def put_target(dst):
        for comp in range(3):

            def put(half, value, comp=comp):
                dst[0, comp, half, pl.ds(8, 16)] = value

            halve(lambda p, rows, comp=comp: res[comp, own_plane + p, rows], 8, put)

    sweep_near(ua, va, ub, vb)
    residual(ub, vb)
    put_target(t_1)
    start(M_T)
    for comp in range(3):
        uc[comp, planes_own, own_rows] = ub[comp, planes_own, own_rows]
    u_fields = [(load_of(ub, 0), 3), (load_of(ub, 1), 3), (load_of(ub, 2), 3)]
    pack(u_fields, u_pack, u_diag_pack)
    start(M_U)

    def repack(load, rows, emit):
        for half in range(2):
            low, high = load(b, half, rows), load(1 - b, half, rows)
            emit(1 + half, jnp.where(even, low, roll(high, 1)))
            emit(3 + half, jnp.where(even, roll(low, -1), high))

    def wrap_after(value):
        return jnp.where(even, roll(value, -1), 0.0)

    def wrap_before(value):
        return jnp.where(even, 0.0, roll(value, 1))

    received(M_KC)

    def put_kq(q, value):
        k_q[q, pl.ds(2, 28)] = value

    repack(lambda slot, half, rows: kc[slot, half, rows], pl.ds(2, 28), put_kq)
    for q in range(1, 5):
        k = k_q[q, pl.ds(2, 28)]
        left, right = z_pair(k, coarse_w, 2)
        czu[0, q, pl.ds(2, 28)] = k + (left + right)
    whole = pl.ds(3, 26)
    for q in range(1, 5):
        ctv[0, q, whole] = czu[0, q, whole] + 0.5 * (czu[0, q, pl.ds(2, 26)] + czu[0, q, pl.ds(4, 26)])
    ctv[0, 5, whole] = wrap_after(ctv[0, 1, whole])
    ctv[0, 0, whole] = wrap_before(ctv[0, 4, whole])
    for q in range(1, 5):
        k = k_q[q, whole]
        t = ctv[0, q, whole] + 0.5 * (ctv[0, q - 1, whole] + ctv[0, q + 1, whole])
        g_q[q, whole] = 16.0 * k + 2.0 * t
        s_q[q, whole] = jnp.where(k > 0.0, 0.3 / jnp.where(k > 0.0, 6.0 * k + t, 1.0), 0.0)

    def coarse_sweep(field, scaled, out_u, out_v, r0, n):
        z_stage(field, scaled, czu, czv, cdz, 1, 4, r0 - 1, n + 2, coarse_w, 2)
        y_stage(field, czu, czv, cdz, cep, cem, cec, ctv, 1, 4, r0, n)
        rows = pl.ds(r0, n)
        for comp in range(3):
            cep[comp, 5, rows] = wrap_after(cep[comp, 1, rows])
            cem[comp, 0, rows] = wrap_before(cem[comp, 4, rows])
            ctv[comp, 5, rows] = wrap_after(ctv[comp, 1, rows])
            ctv[comp, 0, rows] = wrap_before(ctv[comp, 4, rows])
        here = pl.ds(1, 4)
        k, g2, s = k_q[here, rows], g_q[here, rows], s_q[here, rows]
        for comp in range(3):
            terms = x_terms(field, k, g2, cep, cem, cec, ctv, comp, 1, 4, rows)
            u = field[comp, here, rows] + (w_q[comp, here, rows] + s * terms)
            out_u[comp, here, rows] = u
            if out_v is not None:
                out_v[comp, here, rows] = u * k

    def coarse(target, r0, n):
        rows = pl.ds(r0, n)
        for comp in range(3):

            def put(q, value, comp=comp):
                w = 8.0 * s_q[q, rows] * value
                w_q[comp, q, rows] = w
                ca[comp, q, rows] = w
                cva[comp, q, rows] = w * k_q[q, rows]

            repack(lambda slot, half, at, comp=comp: target[slot, comp, half, at], rows, put)
        coarse_sweep(ca, cva, cb, cvb, r0 + 1, n - 2)
        coarse_sweep(cb, cvb, ca, cva, r0 + 2, n - 4)
        coarse_sweep(ca, cva, cb, None, r0 + 3, n - 6)
        last, count = r0 + 3, n - 6
        for comp in range(3):
            for q in range(1, 5):
                value = cb[comp, q, pl.ds(last, count)]
                for x, part in ((q - 1, jnp.where(even, value, roll(value, 1))), (q + 3, jnp.where(even, roll(value, -1), value))):
                    prolonged[comp, x, pl.ds(2 * last - 8, count, stride=2)] = part
                    prolonged[comp, x, pl.ds(2 * last - 7, count, stride=2)] = part

    def correct(field, out_u, out_v, p, m, r0, n):
        rows = pl.ds(r0, n)
        for q in range(m):
            at = p + q
            x = (at - 1 + 5 * b) // 2
            k, free = k_f[at, rows], free_f[at, rows]
            for comp in range(3):
                u = field[comp, at, rows] + free * prolonged[comp, x, rows]
                out_u[comp, at, rows] = u
                out_v[comp, at, rows] = u * k

    received(M_T)
    coarse(t_1, 3, 26)
    received(M_U)
    unpack([(store_of(uc, 0), 3), (store_of(uc, 1), 3), (store_of(uc, 2), 3)], u_land, u_diag_land)
    correct(uc, ud, vd, 1, 11, 5, 38)
    sweep_wide(ud, vd, ue, ve)

    sweep_near(ue, ve, ud, vd)
    residual(ud, vd)
    put_target(t_2)
    start(M_T2)
    received(M_T2)
    coarse(t_2, 4, 24)
    correct(ud, ue, ve, 1 + 2 * b, 9, 7, 34)
    fine(ue, ve, 1 + 2 * b, 9, own_plane, 8, 8, 32, sweep_to(out_f, None))
    result = pltpu.make_async_copy(out_f.at[:, planes_own, own_rows], out_hbm, in_sem.at[3])
    result.start()
    sent(M_IN, M_FACE_U, M_FACE_K, M_FACE_FREE, M_KC, M_T, M_U, M_T2)
    result.wait()


def solution(mesh):
    bricks = mesh.shape["brick"]

    def body(stiffness, prescribed, pinned):
        def f32(*shape):
            return pltpu.VMEM(shape, jnp.float32)

        one, three = f32(PLANES, ROWS, 128), f32(3, PLANES, ROWS, 128)
        q1, q3 = f32(6, COARSE_ROWS, 128), f32(3, 6, COARSE_ROWS, 128)
        scratch = [
            f32(3, 8, 32, 128),
            pltpu.VMEM((8, 32, 128), jnp.int32),
            f32(8, 32, 128),
            *[one] * 5,
            *[three] * 11,
            *[three] * 7,
            f32(3, 8, ROWS, 128),
            *[f32(2, 96, 128)] * 2,
            *[f32(2, 40, 128)] * 2,
            *[f32(2, 72, 128)] * 2,
            *[f32(2, 32, 128)] * 2,
            f32(2, 2, COARSE_ROWS, 128),
            *[f32(2, 3, 2, COARSE_ROWS, 128)] * 2,
            *[q1] * 3,
            *[q3] * 5,
            *[q3] * 7,
            pltpu.SemaphoreType.DMA((4,)),
            pltpu.SemaphoreType.DMA((MESSAGES, 5)),
            pltpu.SemaphoreType.DMA((MESSAGES, 5)),
        ]
        hbm = pl.BlockSpec(memory_space=pl.ANY)
        return pl.pallas_call(
            functools.partial(kernel, bricks),
            out_shape=jax.ShapeDtypeStruct(prescribed.shape, jnp.float32),
            in_specs=[hbm] * 3,
            out_specs=hbm,
            scratch_shapes=scratch,
            compiler_params=pltpu.CompilerParams(collective_id=0, has_side_effects=True, vmem_limit_bytes=58 * 2**20),
        )(stiffness, prescribed, pinned)

    return jax.shard_map(
        body,
        mesh=mesh,
        in_specs=(P("band", "brick", None), P(None, "band", "brick", None), P("band", "brick", None)),
        out_specs=P(None, "band", "brick", None),
        check_vma=False,
    )
```

time: 43.7 us -> 35.5 us (0.81)
  Pallas kernels: 41.4 us -> 33.3 us
    pallas_call x1, Pallas kernels: 41.4 us -> 33.3 us  [body(): pl.pallas_call(functools.partial(kernel, bricks), out_shape=jax.ShapeDtyp...]
where the time goes in v1:
time: 35.5 us; the launch traced here: 35 us
  Pallas kernels  33.3 us (94%)
  local copies, waits for them, and re-layouts  1.77 us (5%)
    pallas_call x1, Pallas kernels, body(): pl.pallas_call(functools.partial(kernel, bricks), out_shape=jax.ShapeDtyp...  33.3 us
    unnamed x1, local copies, waits for them, and re-layouts  1.77 us

profile of v1, /device:TPU:32, one launch (start us, length us, event | category | flops | bytes accessed | tf_op | source)
XLA Modules:
  0.0 35.0 jit_solution(15038819288410553107)
XLA Ops:
  0.0 33.3 %shard_map.37 = f32[3,8,32,128]{3,2,1,0:T(8,128)} custom-call(f32[8,32,128]{2,1,0:T(8,128)} %stiff_in.1, f32[3,8,32,128]{3,2,1,0:T(8,128)} %pres_in.1, s32[8,32,128]{2,1,0:T(8,128)} %pin_in.1), custom_call_target="tpu_custom_call" | custom-call | tf_op jit(solution)/shard_map/pallas_call | solution.py:565
  33.3 1.8 %copy.5 = f32[3,8,32,128]{3,2,1,0:T(8,128)} copy(f32[3,8,32,128]{3,2,1,0:T(8,128)} %shard_map.37) | data formatting | bytes 786432

commit v2 on v1

--- a/solution.py
+++ b/solution.py
@@ -13,8 +13,8 @@
 COARSE_ROWS = 32
 CHUNK = 2
 BAND, UP, DOWN, DIAG_UP, DIAG_DOWN = range(5)
-MESSAGES = 8
-M_IN, M_FACE_U, M_FACE_K, M_FACE_FREE, M_KC, M_T, M_U, M_T2 = range(MESSAGES)
+MESSAGES = 10
+M_IN, M_FACE_U, M_FACE_K, M_FACE_FREE, M_KC, M_LATE_K, M_LATE_FREE, M_T, M_U, M_T2 = range(MESSAGES)
 
 
 def lane_iota():
@@ -30,28 +30,31 @@
     return roll(value, step) * low, roll(value, -step) * high
 
 
-def z_stage(field, scaled, zu, zv, dz, p, m, r0, n, weights, step):
+def z_stage(field, scaled, work, p, m, r0, n, weights, step):
+    zu, zv, dz = work[:3]
     planes, rows = pl.ds(p, m), pl.ds(r0, n)
     for c in range(3):
         u = field[c, planes, rows]
         left, right = z_pair(u, weights, step)
         zu[c, planes, rows] = u + (left + right)
-        dz[c, planes, rows] = 0.5 * (right - left)
+        dz[c, planes, rows] = right - left
     for c in range(3):
         v = scaled[c, planes, rows]
         left, right = z_pair(v, weights, step)
         zv[c, planes, rows] = v + (left + right)
 
 
-def y_stage(field, zu, zv, dz, ep, em, ec, tv, p, m, r0, n):
+def y_stage(field, work, p, m, r0, n):
+    zu, zv, dz, ep, em, ec, tv = work
     planes, mid, low, high = pl.ds(p, m), pl.ds(r0, n), pl.ds(r0 - 1, n), pl.ds(r0 + 1, n)
     for c in range(3):
-        a = zu[c, planes, mid] + 0.5 * (zu[c, planes, low] + zu[c, planes, high])
+        a = zu[c, planes, mid]
+        a = (a + a) + (zu[c, planes, low] + zu[c, planes, high])
         twice = a + a
         if c == 0:
-            g = 0.25 * (field[1, planes, high] - field[1, planes, low]) + dz[2, planes, mid]
+            g = 0.5 * (field[1, planes, high] - field[1, planes, low]) + dz[2, planes, mid]
         elif c == 1:
-            g = 0.25 * (field[0, planes, high] - field[0, planes, low])
+            g = 0.5 * (field[0, planes, high] - field[0, planes, low])
             twice = twice + (dz[2, planes, high] - dz[2, planes, low])
         else:
             g = dz[0, planes, mid]
@@ -59,15 +62,16 @@
         ep[c, planes, mid] = a + g
         em[c, planes, mid] = a - g
         ec[c, planes, mid] = twice
-        tv[c, planes, mid] = zv[c, planes, mid] + 0.5 * (zv[c, planes, low] + zv[c, planes, high])
-
-
-def x_terms(field, k, g2, ep, em, ec, tv, c, p, m, rows):
+        v = zv[c, planes, mid]
+        tv[c, planes, mid] = (v + v) + (zv[c, planes, low] + zv[c, planes, high])
+
+
+def x_terms(field, k, g4, work, c, p, m, rows):
+    ep, em, ec, tv = work[3:]
     here, before, after = pl.ds(p, m), pl.ds(p - 1, m), pl.ds(p + 1, m)
     e = (ep[c, after, rows] + em[c, before, rows]) + ec[c, here, rows]
-    mid = tv[c, here, rows]
-    t = (tv[c, after, rows] + tv[c, before, rows]) + (mid + mid)
-    return t + k * e - g2 * field[c, here, rows]
+    pairs = tv[c, pl.ds(p - 1, m + 1), rows] + tv[c, pl.ds(p, m + 1), rows]
+    return (pairs[:-1] + pairs[1:]) + k * e - g4 * field[c, here, rows]
 
 
 def kernel(
@@ -82,7 +86,7 @@
     k_f,
     free_f,
     fr8_f,
-    g2_f,
+    g4_f,
     fh_f,
     ua,
     va,
@@ -95,44 +99,32 @@
     ve,
     res,
     out_f,
-    zu,
-    zv,
-    dz,
-    ep,
-    em,
-    ec,
-    tv,
-    prolonged,
-    in_pack,
-    in_land,
-    in_diag_pack,
-    in_diag_land,
-    u_pack,
-    u_land,
-    u_diag_pack,
-    u_diag_land,
-    kc,
-    t_1,
-    t_2,
-    k_q,
-    g_q,
-    s_q,
-    w_q,
-    ca,
-    cva,
-    cb,
-    cvb,
-    czu,
-    czv,
-    cdz,
-    cep,
-    cem,
-    cec,
-    ctv,
-    in_sem,
-    send_sem,
-    recv_sem,
+    *rest,
 ):
+    work, work_2, rest = rest[:7], rest[7:14], rest[14:]
+    (
+        prolonged,
+        in_pack,
+        in_land,
+        in_diag_pack,
+        in_diag_land,
+        u_pack,
+        u_land,
+        u_diag_pack,
+        u_diag_land,
+        kc,
+        t_1,
+        t_2,
+        k_q,
+        g_q,
+        s_q,
+        w_q,
+        ca,
+        cva,
+        cb,
+        cvb,
+    ) = rest[:-10]
+    coarse_work, (in_sem, send_sem, recv_sem) = rest[-10:-3], rest[-3:]
     b = lax.axis_index("band")
     i = lax.axis_index("brick")
     has_up, has_down = i > 0, i < bricks - 1
@@ -184,7 +176,7 @@
 
     outer = 12 * b
     k_f[outer] = jnp.zeros((ROWS, 128), jnp.float32)
-    for ref in (ep, em, tv):
+    for ref in (*work[3:5], work[6], *work_2[3:5], work_2[6]):
         for comp in range(3):
             ref[comp, outer] = jnp.zeros((ROWS, 128), jnp.float32)
 
@@ -242,17 +234,20 @@
 
     packed_messages(M_IN, in_pack, in_land, in_diag_pack, in_diag_land)
     face_message(M_FACE_U, ua, 2, True)
-    face_message(M_FACE_K, k_f, 3, False)
-    face_message(M_FACE_FREE, free_f, 3, False)
+    face_message(M_FACE_K, k_f, 2, False)
+    face_message(M_FACE_FREE, free_f, 1, False)
+    third, outer_two = pl.ds(1 + 10 * b, 1), pl.ds(1 + 9 * b, 2)
+    prepare(M_LATE_K, BAND, k_f.at[pl.ds(6, 1), pl.ds(8, 32)], k_f.at[third, pl.ds(8, 32)])
+    prepare(M_LATE_FREE, BAND, free_f.at[pl.ds(6 - b, 2), pl.ds(8, 32)], free_f.at[outer_two, pl.ds(8, 32)])
     coarse_messages(M_KC, kc)
     coarse_messages(M_T, t_1)
     coarse_messages(M_T2, t_2)
     packed_messages(M_U, u_pack, u_land, u_diag_pack, u_diag_land)
     face_message(M_U, uc, 3, True)
 
-    def each(messages, act, above, below):
+    def each(messages, act, above, below, far=True, near=True):
         for holds, kinds in ((above, (UP, DIAG_UP)), (below, (DOWN, DIAG_DOWN))):
-            found = [copies[m, kind] for m in messages for kind in kinds if (m, kind) in copies]
+            found = [copies[m, kind] for m in messages for kind in kinds if far and (m, kind) in copies]
             if found:
 
                 @pl.when(holds)
@@ -261,14 +256,14 @@
                         act(copy)
 
         for m in messages:
-            if (m, BAND) in copies:
+            if near and (m, BAND) in copies:
                 act(copies[m, BAND])
 
     def start(*messages):
         each(messages, lambda copy: copy.start(), has_up, has_down)
 
-    def received(*messages):
-        each(messages, lambda copy: copy.wait_recv(), has_down, has_up)
+    def received(*messages, far=True, near=True):
+        each(messages, lambda copy: copy.wait_recv(), has_down, has_up, far, near)
 
     def sent(*messages):
         each(messages, lambda copy: copy.wait_send(), has_up, has_down)
@@ -339,74 +334,128 @@
     halve(lambda p, rows: k_own[p, rows], 0, put_kc)
 
     pl.semaphore_wait(barrier, 1 + 2 * has_up.astype(jnp.int32) + 2 * has_down.astype(jnp.int32))
-    start(M_IN, M_FACE_U, M_FACE_K, M_FACE_FREE)
-    start(M_KC)
+    start(M_IN, M_KC, M_FACE_U, M_FACE_K, M_FACE_FREE, M_LATE_K, M_LATE_FREE)
+
+    kz, ky = prolonged.at[0], prolonged.at[1]
+
+    def k_z(p, m, r0, n):
+        planes, rows = pl.ds(p, m), pl.ds(r0, n)
+        k = k_f[planes, rows]
+        left, right = z_pair(k, fine_w, 1)
+        kz[planes, rows] = k + (left + right)
+
+    def k_y(p, m, r0, n):
+        planes = pl.ds(p, m)
+        ky[planes, pl.ds(r0, n)] = kz[planes, pl.ds(r0, n)] + 0.5 * (
+            kz[planes, pl.ds(r0 - 1, n)] + kz[planes, pl.ds(r0 + 1, n)]
+        )
+
+    def coefficients(p, m, r0, n):
+        for q in range(0, m, CHUNK):
+            size = min(CHUNK, m - q)
+            at, rows = p + q, pl.ds(r0, n)
+            here = pl.ds(at, size)
+            k, free = k_f[here, rows], free_f[here, rows]
+            t = ky[here, rows] + 0.5 * (ky[pl.ds(at - 1, size), rows] + ky[pl.ds(at + 1, size), rows])
+            g4_f[here, rows] = 32.0 * k + 4.0 * t
+            fr8_f[here, rows] = 0.03125 * free
+            inside = k > 0.0
+            fh_f[here, rows] = jnp.where(inside, 0.15 * free / jnp.where(inside, 6.0 * k + t, 1.0), 0.0)
+
+    def x_stage(field, used, p, m, r0, n, emit):
+        rows, here = pl.ds(r0, n), pl.ds(p, m)
+        k, g4 = k_f[here, rows], g4_f[here, rows]
+        for comp in range(3):
+            emit(comp, here, rows, k, field, x_terms(field, k, g4, used, comp, p, m, rows))
+
+    def fine(field, scaled, m, out_m, r0, n, emit, before=None):
+        first = 1 - b
+        done = 0
+
+        def start_of(q, size):
+            return (1 + q) * first + (12 - q - size) * b
+
+        for q in range(0, m, CHUNK):
+            if before is not None and before[0] == q:
+                before[1]()
+            size = min(CHUNK, m - q)
+            z_stage(field, scaled, work, start_of(q, size), size, r0 - 1, n + 2, fine_w, 1)
+            y_stage(field, work, start_of(q, size), size, r0, n)
+            while done < out_m:
+                out_size = min(CHUNK, out_m - done)
+                if q + size < min(m, done + out_size + 1):
+                    break
+                x_stage(field, work, start_of(done, out_size), out_size, r0, n, emit)
+                done += out_size
+
+    def sweep_to(out_u, out_v):
+        def emit(comp, here, rows, k, field, terms):
+            u = field[comp, here, rows] + fh_f[here, rows] * terms
+            out_u[comp, here, rows] = u
+            if out_v is not None:
+                out_v[comp, here, rows] = u * k
+
+        return emit
+
+    def to_residual(comp, here, rows, k, field, terms):
+        res[comp, here, rows] = fr8_f[here, rows] * terms
+
+    for ref in (kz, ky):
+        ref[outer] = jnp.zeros((ROWS, 128), jnp.float32)
+    all_but_1, all_but_2 = own_plane + b, own_plane + 2 * b
+    halo_2, across_2, last_2 = 9 - 7 * b, 8 - 5 * b, 7 - 3 * b
+    first_sweep = sweep_to(ub, vb)
+    k_z(own_plane, 8, 8, 32)
+    k_y(own_plane, 8, 9, 30)
+    coefficients(all_but_1, 7, 9, 30)
+    for q in range(0, 8, CHUNK):
+        z_stage(ua, va, work, own_plane + q, CHUNK, 8, 32, fine_w, 1)
+        y_stage(ua, work, own_plane + q, CHUNK, 9, 30)
+    for q in range(7):
+        x_stage(ua, work, all_but_1 + q, 1, 9, 30, first_sweep)
+    for q in range(7):
+        z_stage(ub, vb, work_2, all_but_1 + q, 1, 9, 30, fine_w, 1)
+        y_stage(ub, work_2, all_but_1 + q, 1, 10, 28)
+    for q in range(0, 6, CHUNK):
+        x_stage(ub, work_2, all_but_2 + q, CHUNK, 10, 28, to_residual)
+
     received(M_IN, M_FACE_U, M_FACE_K, M_FACE_FREE)
     unpack(
         [(store_of(ua, 0), 2), (store_of(ua, 1), 2), (store_of(ua, 2), 2), (store_of(k_f), 3), (store_of(free_f), 3)],
         in_land,
         in_diag_land,
     )
-    near = pl.ds(6, 36)
-    for q in range(10):
-        at = 1 + b + q
-        k = k_f[at, near]
-        for comp in range(3):
-            va[comp, at, near] = k * ua[comp, at, near]
-
-    for p in range(1, 12):
-        k = k_f[p, pl.ds(5, 38)]
-        left, right = z_pair(k, fine_w, 1)
-        zu[0, p, pl.ds(5, 38)] = k + (left + right)
-        fr8_f[p, own_rows] = 0.0625 * free_f[p, own_rows]
-    for p in range(1, 12):
-        tv[0, p, near] = zu[0, p, near] + 0.5 * (zu[0, p, pl.ds(5, 36)] + zu[0, p, pl.ds(7, 36)])
-    for q in range(10):
-        p = 1 + b + q
-        k = k_f[p, near]
-        t = tv[0, p, near] + 0.5 * (tv[0, p - 1, near] + tv[0, p + 1, near])
-        g2_f[p, near] = 16.0 * k + 2.0 * t
-        diagonal = 6.0 * k + t
-        fh_f[p, near] = jnp.where(k > 0.0, 0.3 * free_f[p, near] / jnp.where(k > 0.0, diagonal, 1.0), 0.0)
-
-    def fine(field, scaled, p, m, out_p, out_m, r0, n, emit):
-        rows = pl.ds(r0, n)
-        done = 0
-        for q in range(0, m, CHUNK):
-            size = min(CHUNK, m - q)
-            z_stage(field, scaled, zu, zv, dz, p + q, size, r0 - 1, n + 2, fine_w, 1)
-            y_stage(field, zu, zv, dz, ep, em, ec, tv, p + q, size, r0, n)
-            while done < out_m:
-                out_size = min(CHUNK, out_m - done)
-                if q + size < min(m, done + out_size + 2):
-                    break
-                at = out_p + done
-                here = pl.ds(at, out_size)
-                k, g2 = k_f[here, rows], g2_f[here, rows]
-                for comp in range(3):
-                    emit(comp, here, rows, k, field, x_terms(field, k, g2, ep, em, ec, tv, comp, at, out_size, rows))
-                done += out_size
-
-    def sweep_to(out_u, out_v):
-        def emit(comp, here, rows, k, field, terms):
-            u = field[comp, here, rows] + fh_f[here, rows] * terms
-            out_u[comp, here, rows] = u
-            if out_v is not None:
-                out_v[comp, here, rows] = u * k
-
-        return emit
-
-    def to_residual(comp, here, rows, k, field, terms):
-        res[comp, here, rows] = fr8_f[here, rows] * terms
-
-    def sweep_wide(field, scaled, out_u, out_v):
-        fine(field, scaled, 1, 11, 1 + b, 10, 6, 36, sweep_to(out_u, out_v))
-
-    def sweep_near(field, scaled, out_u, out_v):
-        fine(field, scaled, 1 + b, 10, 1 + 2 * b, 9, 7, 34, sweep_to(out_u, out_v))
-
-    def residual(field, scaled):
-        fine(field, scaled, 1 + 2 * b, 9, own_plane, 8, 8, 32, to_residual)
+
+    def scale(p, m, r0, n):
+        planes, rows = pl.ds(p, m), pl.ds(r0, n)
+        k = k_f[planes, rows]
+        for comp in range(3):
+            va[comp, planes, rows] = k * ua[comp, planes, rows]
+
+    def strips(act, p, m, low, high, n):
+        act(p, m, low, n)
+        act(p, m, high, n)
+
+    strips(scale, own_plane, 8, 6, 40, 2)
+    scale(halo_2, 2, 6, 36)
+    strips(k_z, own_plane, 8, 6, 40, 2)
+    k_z(halo_2, 2, 6, 36)
+    strips(k_y, own_plane, 8, 7, 39, 2)
+    k_y(halo_2, 2, 7, 34)
+    strips(coefficients, all_but_1, 7, 7, 39, 2)
+    coefficients(across_2, 2, 7, 34)
+    strips(lambda p, m, r0, n: z_stage(ua, va, work, p, m, r0, n, fine_w, 1), own_plane, 8, 6, 40, 2)
+    z_stage(ua, va, work, halo_2, 2, 6, 36, fine_w, 1)
+    strips(lambda p, m, r0, n: y_stage(ua, work, p, m, r0, n), own_plane, 8, 7, 39, 2)
+    y_stage(ua, work, halo_2, 2, 7, 34)
+    strips(lambda p, m, r0, n: x_stage(ua, work, p, m, r0, n, first_sweep), all_but_1, 7, 7, 39, 2)
+    x_stage(ua, work, across_2, 2, 7, 34, first_sweep)
+    strips(lambda p, m, r0, n: z_stage(ub, vb, work_2, p, m, r0, n, fine_w, 1), all_but_1, 7, 7, 39, 2)
+    z_stage(ub, vb, work_2, across_2, 2, 7, 34, fine_w, 1)
+    strips(lambda p, m, r0, n: y_stage(ub, work_2, p, m, r0, n), all_but_1, 7, 8, 38, 2)
+    y_stage(ub, work_2, across_2, 2, 8, 32)
+    strips(lambda p, m, r0, n: x_stage(ub, work_2, p, m, r0, n, to_residual), all_but_2, 6, 8, 38, 2)
+    x_stage(ub, work_2, last_2, 2, 8, 32, to_residual)
 
     def put_target(dst):
         for comp in range(3):
@@ -416,8 +465,6 @@
 
             halve(lambda p, rows, comp=comp: res[comp, own_plane + p, rows], 8, put)
 
-    sweep_near(ua, va, ub, vb)
-    residual(ub, vb)
     put_target(t_1)
     start(M_T)
     for comp in range(3):
@@ -438,12 +485,20 @@
     def wrap_before(value):
         return jnp.where(even, 0.0, roll(value, 1))
 
+    received(M_LATE_K, M_LATE_FREE)
+    for q in range(0, 11, CHUNK):
+        size = min(CHUNK, 11 - q)
+        k_z(1 + q, size, 5, 38)
+        k_y(1 + q, size, 6, 36)
+    coefficients(1 + b, 10, 6, 36)
+
     received(M_KC)
 
     def put_kq(q, value):
         k_q[q, pl.ds(2, 28)] = value
 
     repack(lambda slot, half, rows: kc[slot, half, rows], pl.ds(2, 28), put_kq)
+    czu, ctv = coarse_work[0], coarse_work[6]
     for q in range(1, 5):
         k = k_q[q, pl.ds(2, 28)]
         left, right = z_pair(k, coarse_w, 2)
@@ -456,12 +511,13 @@
     for q in range(1, 5):
         k = k_q[q, whole]
         t = ctv[0, q, whole] + 0.5 * (ctv[0, q - 1, whole] + ctv[0, q + 1, whole])
-        g_q[q, whole] = 16.0 * k + 2.0 * t
-        s_q[q, whole] = jnp.where(k > 0.0, 0.3 / jnp.where(k > 0.0, 6.0 * k + t, 1.0), 0.0)
+        g_q[q, whole] = 32.0 * k + 4.0 * t
+        s_q[q, whole] = jnp.where(k > 0.0, 0.15 / jnp.where(k > 0.0, 6.0 * k + t, 1.0), 0.0)
 
     def coarse_sweep(field, scaled, out_u, out_v, r0, n):
-        z_stage(field, scaled, czu, czv, cdz, 1, 4, r0 - 1, n + 2, coarse_w, 2)
-        y_stage(field, czu, czv, cdz, cep, cem, cec, ctv, 1, 4, r0, n)
+        z_stage(field, scaled, coarse_work, 1, 4, r0 - 1, n + 2, coarse_w, 2)
+        y_stage(field, coarse_work, 1, 4, r0, n)
+        cep, cem, _, ctv = coarse_work[3:]
         rows = pl.ds(r0, n)
         for comp in range(3):
             cep[comp, 5, rows] = wrap_after(cep[comp, 1, rows])
@@ -469,9 +525,9 @@
             ctv[comp, 5, rows] = wrap_after(ctv[comp, 1, rows])
             ctv[comp, 0, rows] = wrap_before(ctv[comp, 4, rows])
         here = pl.ds(1, 4)
-        k, g2, s = k_q[here, rows], g_q[here, rows], s_q[here, rows]
-        for comp in range(3):
-            terms = x_terms(field, k, g2, cep, cem, cec, ctv, comp, 1, 4, rows)
+        k, g4, s = k_q[here, rows], g_q[here, rows], s_q[here, rows]
+        for comp in range(3):
+            terms = x_terms(field, k, g4, coarse_work, comp, 1, 4, rows)
             u = field[comp, here, rows] + (w_q[comp, here, rows] + s * terms)
             out_u[comp, here, rows] = u
             if out_v is not None:
@@ -482,7 +538,7 @@
         for comp in range(3):
 
             def put(q, value, comp=comp):
-                w = 8.0 * s_q[q, rows] * value
+                w = 16.0 * s_q[q, rows] * value
                 w_q[comp, q, rows] = w
                 ca[comp, q, rows] = w
                 cva[comp, q, rows] = w * k_q[q, rows]
@@ -512,22 +568,27 @@
 
     received(M_T)
     coarse(t_1, 3, 26)
-    received(M_U)
+    received(M_U, near=False)
     unpack([(store_of(uc, 0), 3), (store_of(uc, 1), 3), (store_of(uc, 2), 3)], u_land, u_diag_land)
-    correct(uc, ud, vd, 1, 11, 5, 38)
-    sweep_wide(ud, vd, ue, ve)
-
-    sweep_near(ue, ve, ud, vd)
-    residual(ud, vd)
+    correct(uc, ud, vd, own_plane, 8, 5, 38)
+
+    def partner_planes():
+        received(M_U, far=False)
+        correct(uc, ud, vd, 9 - 8 * b, 3, 5, 38)
+
+    fine(ud, vd, 11, 10, 6, 36, sweep_to(ue, ve), (8, partner_planes))
+
+    fine(ue, ve, 10, 9, 7, 34, sweep_to(ud, vd))
+    fine(ud, vd, 9, 8, 8, 32, to_residual)
     put_target(t_2)
     start(M_T2)
     received(M_T2)
     coarse(t_2, 4, 24)
     correct(ud, ue, ve, 1 + 2 * b, 9, 7, 34)
-    fine(ue, ve, 1 + 2 * b, 9, own_plane, 8, 8, 32, sweep_to(out_f, None))
+    fine(ue, ve, 9, 8, 8, 32, sweep_to(out_f, None))
     result = pltpu.make_async_copy(out_f.at[:, planes_own, own_rows], out_hbm, in_sem.at[3])
     result.start()
-    sent(M_IN, M_FACE_U, M_FACE_K, M_FACE_FREE, M_KC, M_T, M_U, M_T2)
+    sent(*range(MESSAGES))
     result.wait()
 
 
@@ -546,8 +607,8 @@
             f32(8, 32, 128),
             *[one] * 5,
             *[three] * 11,
-            *[three] * 7,
-            f32(3, 8, ROWS, 128),
+            *[three] * 14,
+            f32(3, PLANES, ROWS, 128),
             *[f32(2, 96, 128)] * 2,
             *[f32(2, 40, 128)] * 2,
             *[f32(2, 72, 128)] * 2,

time: 35.5 us -> 33.4 us (0.941)
  Pallas kernels: 33.3 us -> 31.4 us
    pallas_call x1, Pallas kernels: 33.3 us -> 31.4 us  [body(): pl.pallas_call(functools.partial(kernel, bricks), out_shape=jax.ShapeDtyp...]
where the time goes in v2:
time: 33.4 us; the launch traced here: 33.1 us
  Pallas kernels  31.4 us (94%)
  local copies, waits for them, and re-layouts  1.77 us (5%)
    pallas_call x1, Pallas kernels, body(): pl.pallas_call(functools.partial(kernel, bricks), out_shape=jax.ShapeDtyp...  31.4 us
    unnamed x1, local copies, waits for them, and re-layouts  1.77 us

profile of v2, /device:TPU:32, one launch (start us, length us, event | category | flops | bytes accessed | tf_op | source)
XLA Modules:
  0.0 33.1 jit_solution(1550122231317515226)
XLA Ops:
  0.0 31.4 %shard_map.37 = f32[3,8,32,128]{3,2,1,0:T(8,128)} custom-call(f32[8,32,128]{2,1,0:T(8,128)} %stiff_in.1, f32[3,8,32,128]{3,2,1,0:T(8,128)} %pres_in.1, s32[8,32,128]{2,1,0:T(8,128)} %pin_in.1), custom_call_target="tpu_custom_call" | custom-call | tf_op jit(solution)/shard_map/pallas_call | solution.py:626
  31.4 1.8 %copy.5 = f32[3,8,32,128]{3,2,1,0:T(8,128)} copy(f32[3,8,32,128]{3,2,1,0:T(8,128)} %shard_map.37) | data formatting | bytes 786432

commit v3 on v2

--- a/solution.py
+++ b/solution.py
@@ -13,8 +13,8 @@
 COARSE_ROWS = 32
 CHUNK = 2
 BAND, UP, DOWN, DIAG_UP, DIAG_DOWN = range(5)
-MESSAGES = 10
-M_IN, M_FACE_U, M_FACE_K, M_FACE_FREE, M_KC, M_LATE_K, M_LATE_FREE, M_T, M_U, M_T2 = range(MESSAGES)
+MESSAGES = 12
+M_IN, M_FACE_U, M_FACE_K, M_FACE_FREE, M_KC, M_LATE, M_LATE_K, M_LATE_FREE, M_U, M_T, M_FACE_U1, M_T2 = range(MESSAGES)
 
 
 def lane_iota():
@@ -108,6 +108,10 @@
         in_land,
         in_diag_pack,
         in_diag_land,
+        late_pack,
+        late_land,
+        late_diag_pack,
+        late_diag_land,
         u_pack,
         u_land,
         u_diag_pack,
@@ -115,6 +119,10 @@
         kc,
         t_1,
         t_2,
+        t1_pack,
+        t1_land,
+        t2_pack,
+        t2_land,
         k_q,
         g_q,
         s_q,
@@ -157,14 +165,14 @@
         greet(DIAG_DOWN)
 
     def outside(slot, rows):
-        for ref in (in_land, in_diag_land, u_land, u_diag_land):
+        for ref in (in_land, in_diag_land, late_land, late_diag_land, u_land, u_diag_land):
             ref[slot] = jnp.zeros(ref.shape[1:], jnp.float32)
+        for ref in (t1_land, t2_land):
+            for band in range(2):
+                ref[slot, band] = jnp.zeros(ref.shape[2:], jnp.float32)
         for band in range(2):
             for half in range(2):
                 kc[band, half, rows] = jnp.zeros((8, 128), jnp.float32)
-                for comp in range(3):
-                    t_1[band, comp, half, rows] = jnp.zeros((8, 128), jnp.float32)
-                    t_2[band, comp, half, rows] = jnp.zeros((8, 128), jnp.float32)
 
     @pl.when(jnp.logical_not(has_up))
     def _():
@@ -222,15 +230,19 @@
 
     def coarse_messages(message, ref):
         def at(band, start, count):
-            if len(ref.shape) == 4:
-                return ref.at[band, :, pl.ds(start, count)]
-            return ref.at[band, :, :, pl.ds(start, count)]
+            return ref.at[band, :, pl.ds(start, count)]
 
         prepare(message, BAND, at(0, 8, 16), at(1, 8, 16))
         prepare(message, UP, at(0, 8, 8), at(0, 24, 8))
         prepare(message, DIAG_UP, at(0, 8, 8), at(1, 24, 8))
         prepare(message, DOWN, at(0, 16, 8), at(0, 0, 8))
         prepare(message, DIAG_DOWN, at(0, 16, 8), at(1, 0, 8))
+
+    def target_messages(message, ref, packed, land):
+        prepare(message, BAND, ref.at[0, :, :, pl.ds(8, 16)], ref.at[1, :, :, pl.ds(8, 16)])
+        for slot, same, other in ((0, UP, DIAG_UP), (1, DOWN, DIAG_DOWN)):
+            prepare(message, same, packed.at[slot], land.at[slot, 0])
+            prepare(message, other, packed.at[slot], land.at[slot, 1])
 
     packed_messages(M_IN, in_pack, in_land, in_diag_pack, in_diag_land)
     face_message(M_FACE_U, ua, 2, True)
@@ -240,14 +252,15 @@
     prepare(M_LATE_K, BAND, k_f.at[pl.ds(6, 1), pl.ds(8, 32)], k_f.at[third, pl.ds(8, 32)])
     prepare(M_LATE_FREE, BAND, free_f.at[pl.ds(6 - b, 2), pl.ds(8, 32)], free_f.at[outer_two, pl.ds(8, 32)])
     coarse_messages(M_KC, kc)
-    coarse_messages(M_T, t_1)
-    coarse_messages(M_T2, t_2)
+    target_messages(M_T, t_1, t1_pack, t1_land)
+    target_messages(M_T2, t_2, t2_pack, t2_land)
+    packed_messages(M_LATE, late_pack, late_land, late_diag_pack, late_diag_land)
     packed_messages(M_U, u_pack, u_land, u_diag_pack, u_diag_land)
-    face_message(M_U, uc, 3, True)
-
-    def each(messages, act, above, below, far=True, near=True):
+    face_message(M_FACE_U1, uc, 3, True)
+
+    def each(messages, act, above, below):
         for holds, kinds in ((above, (UP, DIAG_UP)), (below, (DOWN, DIAG_DOWN))):
-            found = [copies[m, kind] for m in messages for kind in kinds if far and (m, kind) in copies]
+            found = [copies[m, kind] for m in messages for kind in kinds if (m, kind) in copies]
             if found:
 
                 @pl.when(holds)
@@ -256,46 +269,50 @@
                         act(copy)
 
         for m in messages:
-            if near and (m, BAND) in copies:
+            if (m, BAND) in copies:
                 act(copies[m, BAND])
 
     def start(*messages):
         each(messages, lambda copy: copy.start(), has_up, has_down)
 
-    def received(*messages, far=True, near=True):
-        each(messages, lambda copy: copy.wait_recv(), has_down, has_up, far, near)
+    def received(*messages):
+        each(messages, lambda copy: copy.wait_recv(), has_down, has_up)
 
     def sent(*messages):
         each(messages, lambda copy: copy.wait_send(), has_up, has_down)
 
-    def edges(slot, depth):
-        return (pl.ds(8, depth), pl.ds(40, depth)) if slot == 0 else (pl.ds(40 - depth, depth), pl.ds(8 - depth, depth))
-
-    def pack(fields, dst, diag_dst):
-        total = sum(depth for _, depth in fields)
-        face = own_plane + 5 * (1 - b)
+    def edge(slot, depth, skip):
+        if slot == 0:
+            return pl.ds(8 + skip, depth), pl.ds(40 + skip, depth)
+        return pl.ds(40 - skip - depth, depth), pl.ds(8 - skip - depth, depth)
+
+    def pieces(fields, count):
+        total = sum(depth for _, depth, _ in fields)
         for slot in range(2):
             at = 0
-            for load, depth in fields:
-                rows = edges(slot, depth)[0]
-                for q in range(8):
-                    dst[slot, pl.ds(q * total + at, depth)] = load(own_plane + q, rows)
-                for q in range(3):
-                    diag_dst[slot, pl.ds(q * total + at, depth)] = load(face + q, rows)
+            for access, depth, skip in fields:
+                out_rows, in_rows = edge(slot, depth, skip)
+                for q in range(count):
+                    yield slot, q, access, out_rows, in_rows, pl.ds(q * total + at, depth)
                 at += depth
 
-    def unpack(fields, land, diag_land):
-        total = sum(depth for _, depth in fields)
-        face = 1 + 8 * (1 - b)
-        for slot in range(2):
-            at = 0
-            for store, depth in fields:
-                rows = edges(slot, depth)[1]
-                for q in range(8):
-                    store(own_plane + q, rows, land[slot, pl.ds(q * total + at, depth)])
-                for q in range(3):
-                    store(face + q, rows, diag_land[slot, pl.ds(q * total + at, depth)])
-                at += depth
+    def pack(fields, dst):
+        for slot, q, load, rows, _, at in pieces(fields, 8):
+            dst[slot, at] = load(own_plane + q, rows)
+
+    def pack_diag(fields, dst, count):
+        face = own_plane + (8 - count) * (1 - b)
+        for slot, q, load, rows, _, at in pieces(fields, count):
+            dst[slot, at] = load(face + q, rows)
+
+    def unpack(fields, land):
+        for slot, q, store, _, rows, at in pieces(fields, 8):
+            store(own_plane + q, rows, land[slot, at])
+
+    def unpack_diag(fields, land, count):
+        face = (4 - count) * b + 9 * (1 - b)
+        for slot, q, store, _, rows, at in pieces(fields, count):
+            store(face + q, rows, land[slot, at])
 
     def load_of(ref, comp=None):
         return (lambda p, rows: ref[p, rows]) if comp is None else (lambda p, rows: ref[comp, p, rows])
@@ -322,11 +339,22 @@
             u = pr_in[comp, q] * pinned
             ua[comp, at, own_rows] = u
             va[comp, at, own_rows] = k * u
-    pack(
-        [(load_of(ua, 0), 2), (load_of(ua, 1), 2), (load_of(ua, 2), 2), (load_of(k_f), 3), (load_of(free_f), 3)],
-        in_pack,
-        in_diag_pack,
-    )
+    def early(of):
+        return [(of(ua, 0), 2, 0), (of(ua, 1), 2, 0), (of(ua, 2), 2, 0), (of(k_f), 2, 0), (of(free_f), 1, 0)]
+
+    def late(of):
+        return [(of(k_f), 1, 2), (of(free_f), 2, 1)]
+
+    def late_diag(of):
+        return [(of(k_f), 3, 0), (of(free_f), 3, 0)]
+
+    def rows_of_u1(of, ref):
+        return [(of(ref, comp), 3, 0) for comp in range(3)]
+
+    pack(early(load_of), in_pack)
+    pack_diag(early(load_of), in_diag_pack, 2)
+    pack(late(load_of), late_pack)
+    pack_diag(late_diag(load_of), late_diag_pack, 3)
 
     def put_kc(half, value):
         kc[0, half, pl.ds(8, 16)] = 0.125 * value
@@ -334,7 +362,8 @@
     halve(lambda p, rows: k_own[p, rows], 0, put_kc)
 
     pl.semaphore_wait(barrier, 1 + 2 * has_up.astype(jnp.int32) + 2 * has_down.astype(jnp.int32))
-    start(M_IN, M_KC, M_FACE_U, M_FACE_K, M_FACE_FREE, M_LATE_K, M_LATE_FREE)
+    start(M_IN, M_FACE_U, M_FACE_K, M_FACE_FREE)
+    start(M_KC, M_LATE, M_LATE_K, M_LATE_FREE)
 
     kz, ky = prolonged.at[0], prolonged.at[1]
 
@@ -420,11 +449,8 @@
         x_stage(ub, work_2, all_but_2 + q, CHUNK, 10, 28, to_residual)
 
     received(M_IN, M_FACE_U, M_FACE_K, M_FACE_FREE)
-    unpack(
-        [(store_of(ua, 0), 2), (store_of(ua, 1), 2), (store_of(ua, 2), 2), (store_of(k_f), 3), (store_of(free_f), 3)],
-        in_land,
-        in_diag_land,
-    )
+    unpack(early(store_of), in_land)
+    unpack_diag(early(store_of), in_diag_land, 2)
 
     def scale(p, m, r0, n):
         planes, rows = pl.ds(p, m), pl.ds(r0, n)
@@ -450,6 +476,9 @@
     y_stage(ua, work, halo_2, 2, 7, 34)
     strips(lambda p, m, r0, n: x_stage(ua, work, p, m, r0, n, first_sweep), all_but_1, 7, 7, 39, 2)
     x_stage(ua, work, across_2, 2, 7, 34, first_sweep)
+    pack(rows_of_u1(load_of, ub), u_pack)
+    pack_diag(rows_of_u1(load_of, ub), u_diag_pack, 3)
+    start(M_U)
     strips(lambda p, m, r0, n: z_stage(ub, vb, work_2, p, m, r0, n, fine_w, 1), all_but_1, 7, 7, 39, 2)
     z_stage(ub, vb, work_2, across_2, 2, 7, 34, fine_w, 1)
     strips(lambda p, m, r0, n: y_stage(ub, work_2, p, m, r0, n), all_but_1, 7, 8, 38, 2)
@@ -457,21 +486,31 @@
     strips(lambda p, m, r0, n: x_stage(ub, work_2, p, m, r0, n, to_residual), all_but_2, 6, 8, 38, 2)
     x_stage(ub, work_2, last_2, 2, 8, 32, to_residual)
 
-    def put_target(dst):
+    def put_target(dst, packed, depth):
         for comp in range(3):
 
             def put(half, value, comp=comp):
                 dst[0, comp, half, pl.ds(8, 16)] = value
 
             halve(lambda p, rows, comp=comp: res[comp, own_plane + p, rows], 8, put)
-
-    put_target(t_1)
+            for half in range(2):
+                at = pl.ds((2 * comp + half) * depth, depth)
+                packed[0, at] = dst[0, comp, half, pl.ds(8, depth)]
+                packed[1, at] = dst[0, comp, half, pl.ds(24 - depth, depth)]
+
+    def far_target(dst, land, depth):
+        for band in range(2):
+            for comp in range(3):
+                for half in range(2):
+                    at = pl.ds((2 * comp + half) * depth, depth)
+                    dst[band, comp, half, pl.ds(24, depth)] = land[0, band, at]
+                    dst[band, comp, half, pl.ds(8 - depth, depth)] = land[1, band, at]
+
+    put_target(t_1, t1_pack, 5)
     start(M_T)
     for comp in range(3):
         uc[comp, planes_own, own_rows] = ub[comp, planes_own, own_rows]
-    u_fields = [(load_of(ub, 0), 3), (load_of(ub, 1), 3), (load_of(ub, 2), 3)]
-    pack(u_fields, u_pack, u_diag_pack)
-    start(M_U)
+    start(M_FACE_U1)
 
     def repack(load, rows, emit):
         for half in range(2):
@@ -485,7 +524,9 @@
     def wrap_before(value):
         return jnp.where(even, 0.0, roll(value, 1))
 
-    received(M_LATE_K, M_LATE_FREE)
+    received(M_LATE, M_LATE_K, M_LATE_FREE)
+    unpack(late(store_of), late_land)
+    unpack_diag(late_diag(store_of), late_diag_land, 3)
     for q in range(0, 11, CHUNK):
         size = min(CHUNK, 11 - q)
         k_z(1 + q, size, 5, 38)
@@ -567,22 +608,25 @@
                 out_v[comp, at, rows] = u * k
 
     received(M_T)
+    far_target(t_1, t1_land, 5)
     coarse(t_1, 3, 26)
-    received(M_U, near=False)
-    unpack([(store_of(uc, 0), 3), (store_of(uc, 1), 3), (store_of(uc, 2), 3)], u_land, u_diag_land)
+    received(M_U)
+    unpack(rows_of_u1(store_of, uc), u_land)
+    unpack_diag(rows_of_u1(store_of, uc), u_diag_land, 3)
     correct(uc, ud, vd, own_plane, 8, 5, 38)
 
     def partner_planes():
-        received(M_U, far=False)
+        received(M_FACE_U1)
         correct(uc, ud, vd, 9 - 8 * b, 3, 5, 38)
 
     fine(ud, vd, 11, 10, 6, 36, sweep_to(ue, ve), (8, partner_planes))
 
     fine(ue, ve, 10, 9, 7, 34, sweep_to(ud, vd))
     fine(ud, vd, 9, 8, 8, 32, to_residual)
-    put_target(t_2)
+    put_target(t_2, t2_pack, 4)
     start(M_T2)
     received(M_T2)
+    far_target(t_2, t2_land, 4)
     coarse(t_2, 4, 24)
     correct(ud, ue, ve, 1 + 2 * b, 9, 7, 34)
     fine(ue, ve, 9, 8, 8, 32, sweep_to(out_f, None))
@@ -609,12 +653,18 @@
             *[three] * 11,
             *[three] * 14,
             f32(3, PLANES, ROWS, 128),
-            *[f32(2, 96, 128)] * 2,
-            *[f32(2, 40, 128)] * 2,
+            *[f32(2, 72, 128)] * 2,
+            *[f32(2, 24, 128)] * 2,
+            *[f32(2, 24, 128)] * 2,
+            *[f32(2, 24, 128)] * 2,
             *[f32(2, 72, 128)] * 2,
             *[f32(2, 32, 128)] * 2,
             f32(2, 2, COARSE_ROWS, 128),
             *[f32(2, 3, 2, COARSE_ROWS, 128)] * 2,
+            f32(2, 32, 128),
+            f32(2, 2, 32, 128),
+            f32(2, 24, 128),
+            f32(2, 2, 24, 128),
             *[q1] * 3,
             *[q3] * 5,
             *[q3] * 7,

time: 33.4 us -> 32.1 us (0.961)
  Pallas kernels: 31.4 us -> 30.2 us
    pallas_call x1, Pallas kernels: 31.4 us -> 30.2 us  [body(): pl.pallas_call(functools.partial(kernel, bricks), out_shape=jax.ShapeDtyp...]
where the time goes in v3:
time: 32.1 us; the launch traced here: 32 us
  Pallas kernels  30.2 us (94%)
  local copies, waits for them, and re-layouts  1.77 us (6%)
    pallas_call x1, Pallas kernels, body(): pl.pallas_call(functools.partial(kernel, bricks), out_shape=jax.ShapeDtyp...  30.2 us
    unnamed x1, local copies, waits for them, and re-layouts  1.77 us

profile of v3, /device:TPU:32, one launch (start us, length us, event | category | flops | bytes accessed | tf_op | source)
XLA Modules:
  0.0 32.0 jit_solution(6650399613360292881)
XLA Ops:
  0.0 30.2 %shard_map.37 = f32[3,8,32,128]{3,2,1,0:T(8,128)} custom-call(f32[8,32,128]{2,1,0:T(8,128)} %stiff_in.1, f32[3,8,32,128]{3,2,1,0:T(8,128)} %pres_in.1, s32[8,32,128]{2,1,0:T(8,128)} %pin_in.1), custom_call_target="tpu_custom_call" | custom-call | tf_op jit(solution)/shard_map/pallas_call | solution.py:676
  30.2 1.8 %copy.5 = f32[3,8,32,128]{3,2,1,0:T(8,128)} copy(f32[3,8,32,128]{3,2,1,0:T(8,128)} %shard_map.37) | data formatting | bytes 786432

commit v4 on v3

--- a/solution.py
+++ b/solution.py
@@ -338,7 +338,6 @@
         for comp in range(3):
             u = pr_in[comp, q] * pinned
             ua[comp, at, own_rows] = u
-            va[comp, at, own_rows] = k * u
     def early(of):
         return [(of(ua, 0), 2, 0), (of(ua, 1), 2, 0), (of(ua, 2), 2, 0), (of(k_f), 2, 0), (of(free_f), 1, 0)]
 
@@ -353,17 +352,20 @@
 
     pack(early(load_of), in_pack)
     pack_diag(early(load_of), in_diag_pack, 2)
+
+    pl.semaphore_wait(barrier, 1 + 2 * has_up.astype(jnp.int32) + 2 * has_down.astype(jnp.int32))
+    start(M_IN, M_FACE_U, M_FACE_K, M_FACE_FREE)
     pack(late(load_of), late_pack)
     pack_diag(late_diag(load_of), late_diag_pack, 3)
-
     def put_kc(half, value):
         kc[0, half, pl.ds(8, 16)] = 0.125 * value
 
     halve(lambda p, rows: k_own[p, rows], 0, put_kc)
-
-    pl.semaphore_wait(barrier, 1 + 2 * has_up.astype(jnp.int32) + 2 * has_down.astype(jnp.int32))
-    start(M_IN, M_FACE_U, M_FACE_K, M_FACE_FREE)
     start(M_KC, M_LATE, M_LATE_K, M_LATE_FREE)
+    for q in range(8):
+        at = own_plane + q
+        for comp in range(3):
+            va[comp, at, own_rows] = k_own[q] * ua[comp, at, own_rows]
 
     kz, ky = prolonged.at[0], prolonged.at[1]
 

time: 32.1 us -> 32.1 us (level)
  no operation moved by 1% of the time
where the time goes in v4:
time: 32.1 us; the launch traced here: 32 us
  Pallas kernels  30.2 us (94%)
  local copies, waits for them, and re-layouts  1.77 us (6%)
    pallas_call x1, Pallas kernels, body(): pl.pallas_call(functools.partial(kernel, bricks), out_shape=jax.ShapeDtyp...  30.2 us
    unnamed x1, local copies, waits for them, and re-layouts  1.77 us

profile of v4, /device:TPU:32, one launch (start us, length us, event | category | flops | bytes accessed | tf_op | source)
XLA Modules:
  0.0 32.0 jit_solution(15527661269199981622)
XLA Ops:
  0.0 30.2 %shard_map.37 = f32[3,8,32,128]{3,2,1,0:T(8,128)} custom-call(f32[8,32,128]{2,1,0:T(8,128)} %stiff_in.1, f32[3,8,32,128]{3,2,1,0:T(8,128)} %pres_in.1, s32[8,32,128]{2,1,0:T(8,128)} %pin_in.1), custom_call_target="tpu_custom_call" | custom-call | tf_op jit(solution)/shard_map/pallas_call | solution.py:678
  30.2 1.8 %copy.5 = f32[3,8,32,128]{3,2,1,0:T(8,128)} copy(f32[3,8,32,128]{3,2,1,0:T(8,128)} %shard_map.37) | data formatting | bytes 786432
